TPU v7x, 256 devices: a whole 4x4x8 slice. The times are simulated.
256 devices in a mesh: dp: 256 (over z, y, x, core).
Axes of the slice: x: 4, y: 4, z: 8, core: 2. Of those that a mesh axis runs over, the one named last changes fastest.
Arguments:
- left_embed: float32 [18432, 384], P('dp'), may hold values from -6 to 6
- right_embed: float32 [18432, 384], P('dp'), may hold values from -6 to 6
Outputs:
- left_grad: float32 [18432, 384], P('dp')
- right_grad: float32 [18432, 384], P('dp')
- mean_loss: float32 [], replicated
All inputs are finite; a program needn't handle non-finite values.
Results may differ from a plain program's by a relative error of at most 0.0056.
The roundings to bfloat16 on the way count: a program that leaves them out, or rounds other values in their place, can miss the bound.
Values may be sent and summed in bfloat16 or wider, within the bound.
A program may use at most 256 MiB of HBM per device.

v0:
```python
import math

import jax
import jax.numpy as jnp
from jax import lax
from jax.sharding import PartitionSpec as P


def shards(left_embed, right_embed):
    local_rows = left_embed.shape[0]
    width = left_embed.shape[1]
    devices = lax.axis_size("dp")
    offset = lax.axis_index("dp") * local_rows
    inverse_temp = 2.0 / math.sqrt(width)
    left_bf = left_embed.astype(jnp.bfloat16)
    right_bf = right_embed.astype(jnp.bfloat16)
    right_all = lax.all_gather(right_bf, "dp", axis=0, tiled=True)
    scores = (
        lax.dot_general(
            left_bf, right_all, (((1,), (1,)), ((), ())), preferred_element_type=jnp.float32
        )
        * inverse_temp
    )
    row_peak = jnp.max(scores, axis=1)
    row_lse = row_peak + jnp.log(jnp.sum(jnp.exp(scores - row_peak[:, None]), axis=1))
    here = offset + jnp.arange(local_rows, dtype=jnp.int32)
    local_peak = jnp.max(scores, axis=0)
    local_mass = jnp.sum(jnp.exp(scores - local_peak[None, :]), axis=0)
    global_peak = lax.pmax(local_peak.astype(jnp.bfloat16), "dp").astype(local_peak.dtype)
    global_mass = lax.psum(local_mass * jnp.exp(local_peak - global_peak), "dp")
    column_lse = global_peak + jnp.log(global_mass)
    own_scores = lax.dynamic_slice_in_dim(scores, offset, local_rows, 1)
    matched = jnp.diagonal(own_scores)
    column_own = lax.dynamic_slice_in_dim(column_lse, offset, local_rows, 0)
    mean_loss = lax.psum(jnp.sum(row_lse + column_own - 2.0 * matched), "dp") / (
        2.0 * local_rows * devices
    )
    columns = jnp.arange(scores.shape[1], dtype=jnp.int32)
    weights = jnp.exp(scores - row_lse[:, None]) + jnp.exp(scores - column_lse[None, :])
    weights = jnp.where(columns[None, :] == here[:, None], weights - 2.0, weights)
    weights_bf = weights.astype(jnp.bfloat16)
    left_grad = jnp.dot(weights_bf, right_all, preferred_element_type=jnp.float32)
    lse_all = lax.all_gather(row_lse, "dp", axis=0, tiled=True)
    shard_rows = lax.all_gather(left_bf, "dp", axis=0, tiled=True)
    count = shard_rows.shape[0]
    part_scores = (
        lax.dot_general(
            shard_rows, right_bf, (((1,), (1,)), ((), ())), preferred_element_type=jnp.float32
        )
        * inverse_temp
    )
    part_weights = jnp.exp(part_scores - lse_all[:, None]) + jnp.exp(
        part_scores - column_own[None, :]
    )
    sources = jnp.arange(count, dtype=jnp.int32)
    part_weights = jnp.where(sources[:, None] == here[None, :], part_weights - 2.0, part_weights)
    part_bf = part_weights.astype(jnp.bfloat16)
    right_grad = lax.dot_general(
        part_bf, shard_rows, (((0,), (0,)), ((), ())), preferred_element_type=jnp.float32
    )
    return (left_grad, right_grad, mean_loss)


def solution(mesh):
    return jax.shard_map(
        shards,
        mesh=mesh,
        in_specs=(P("dp", None), P("dp", None)),
        out_specs=(P("dp", None), P("dp", None), P()),
        check_vma=False,
    )
```

profile of v0, /device:TPU:1, one launch (start us, length us, event | category | flops | bytes accessed | tf_op | source)
XLA Modules:
  0.0 621.7 jit_solution(8868899919728713002)
XLA Ops:
  7.2 0.0 all-gather.3.cloned.1.call-start
  7.2 1.5 convert_element_type.19
  8.7 0.0 all-gather.3.cloned.1.call-update
  8.8 0.0 all-reduce.4.cloned.1.call-start
  8.8 0.9 convert_element_type.18
  9.7 128.9 %all-gather.3.cloned.1.call-done = bf16[18432,384]{1,0:T(8,128)(2,1)} async-done(((bf16[72,384]{1,0:T(8,128)(2,1)}), bf16[18432,384]{1,0:T(8,128)(2,1)}) %all-gather.3.cloned.1.call-update) | async-done | bytes 14155792 | tf_op jit(solution)/shard_map/all_gather | solution.py:17
  138.7 13.2 %fusion.19 = (f32[72]{0:T(128)S(1)}, f32[18432]{0:T(1024)S(1)}, f32[72,18432]{1,0:T(8,128)}) fusion(bf16[72,384]{1,0:T(8,128)(2,1)S(1)} %convert_element_type.18, bf16[18432,384]{1,0:T(8,128)(2,1)} %all-gather.3.cloned.1.call-done), kind=kOutput, calls=%fused_computation.34 | convolution fusion | flops 1023178688 | bytes 19593504 | tf_op jit(solution)/shard_map/dot_general | solution.py:19
  151.9 74.7 %pmax.7 = bf16[18432]{0:T(1024)(128)(2,1)S(1)} all-reduce(bf16[18432]{0:T(1024)(128)(2,1)S(1)} %convert_element_type.20), channel_id=1, replica_groups=mesh['dp'=256] {'dp'}, use_global_device_ids=true, to_apply=%region_3.0 | all-reduce | flops 18432 | bytes 73728 | tf_op jit(solution)/shard_map/pmax | solution.py:29
  226.7 4.3 exponential_reduce_fusion.1
  230.9 0.7 fusion.15
  231.6 0.1 fusion.20
  231.7 0.6 copy-done.1
  232.3 0.0 all-reduce.4.cloned.1.call-update
  232.4 0.0 all-gather.5.cloned.1.call-start
  232.4 0.7 all-gather.5.cloned.1.call-update
  233.1 1.0 constant_dynamic-slice_fusion
  234.1 1.7 gather_fusion
  235.8 236.0 %all-reduce.4.cloned.1.call-done = (f32[18432]{0:T(1024)}, f32[18432]{0:T(1024)}) async-done(((f32[18432]{0:T(1024)}, f32[18432]{0:T(1024)}), (f32[18432]{0:T(1024)}, f32[18432]{0:T(1024)})) %all-reduce.4.cloned.1.call-update) | async-done | bytes 147472 | tf_op jit(solution)/shard_map/psum | solution.py:30
  471.8 0.9 convert_add_fusion
  472.7 0.7 subtract_reduce_fusion
  473.4 76.3 %psum.15 = f32[]{:T(128)} all-reduce(f32[]{:T(128)} %get-tuple-element.9), channel_id=1, replica_groups=mesh['dp'=256] {'dp'}, use_global_device_ids=true, to_apply=%region_7.8 | all-reduce | flops 1 | bytes 8 | tf_op jit(solution)/shard_map/psum | solution.py:35
  550.4 10.2 %fusion.3 = f32[72,384]{1,0:T(8,128)} fusion(bf16[18432,384]{1,0:T(8,128)(2,1)} %all-gather.3.cloned.1.call-done, f32[72,18432]{1,0:T(8,128)} %get-tuple-element.13, f32[18432]{0:T(1024)S(1)} %convert_add_fusion, f32[72]{0:T(128)S(1)} %get-tuple-element.12, s32[72]{0:T(128)S(1)} %iota_add_fusion), kind=kOutput, calls=%fused_computation.12 | convolution fusion | flops 1028505600 | bytes 19649088 | tf_op jit(solution)/shard_map/dot_general | solution.py:42
  560.6 35.7 %all-gather.5.cloned.1.call-done = bf16[18432,384]{1,0:T(8,128)(2,1)} async-done(((bf16[72,384]{1,0:T(8,128)(2,1)}), bf16[18432,384]{1,0:T(8,128)(2,1)}) %all-gather.5.cloned.1.call-update) | async-done | bytes 14155792 | tf_op jit(solution)/shard_map/all_gather | solution.py:44
  596.2 17.8 %fusion.2 = f32[72,384]{1,0:T(8,128)} fusion(bf16[18432,384]{1,0:T(8,128)(2,1)} %all-gather.5.cloned.1.call-done, bf16[72,384]{1,0:T(8,128)(2,1)S(1)} %copy-done.2, f32[72]{0:T(128)S(1)} %get-tuple-element.10, f32[18432]{0:T(1024)S(1)} %copy-done.3, s32[72]{0:T(128)S(1)} %iota_add_fusion), kind=kOutput, calls=%fused_computation.11 | convolution fusion | flops 2049048576 | bytes 14395968 | tf_op jit(solution)/shard_map/dot_general | solution.py:58
  (11 shorter events, 0.0 us)
Async XLA Ops:
  7.2 131.5 %all-gather.3.cloned.1.call-start = ((), (), s32[]{:S(2)}) async-start(), calls=%async_computation | async-start | bytes 14211072 | tf_op jit(solution)/shard_map/all_gather | solution.py:17
  8.8 463.0 %all-reduce.4.cloned.1.call-start = ((), (), s32[]{:S(2)}) async-start(), calls=%async_computation.2 | async-start | bytes 294912 | tf_op jit(solution)/shard_map/psum | solution.py:30
  9.7 142.2 %copy-start = (bf16[72,384]{1,0:T(8,128)(2,1)}, bf16[72,384]{1,0:T(8,128)(2,1)S(1)}, u32[]{:S(2)}) copy-start(bf16[72,384]{1,0:T(8,128)(2,1)S(1)} %convert_element_type.18) | copy-start | bytes 165892
  231.7 0.6 copy-start.1
  232.4 363.9 %all-gather.5.cloned.1.call-start = ((), (), s32[]{:S(2)}) async-start(), calls=%async_computation.1 | async-start | bytes 14211072 | tf_op jit(solution)/shard_map/all_gather | solution.py:44
  550.3 45.9 %copy-start.2 = (bf16[72,384]{1,0:T(8,128)(2,1)S(1)}, bf16[72,384]{1,0:T(8,128)(2,1)}, u32[]{:S(2)}) copy-start(bf16[72,384]{1,0:T(8,128)(2,1)} %convert_element_type.19) | copy-start | bytes 165892
  550.3 45.9 %copy-start.3 = (f32[18432]{0:T(1024)S(1)}, f32[18432]{0:T(1024)}, u32[]{:S(2)}) copy-start(f32[18432]{0:T(1024)} %get-tuple-element.8) | copy-start | bytes 221188
Sparse Core Ops, SparseCore 0:
  11.7 126.9 all-gather.2
  232.5 239.2 all-reduce.3
  475.5 120.7 all-gather.4
where the time goes:
time: 622 us
  waiting for transfers between devices  401 us (64%)
  blocking collectives  151 us (24%)
  matrix products  41.2 us (7%)
  between operations  15.6 us (3%)
  other arithmetic  9.07 us (1%)
    psum x1, waiting for transfers between devices, shards(): global_mass = lax.psum(local_mass * jnp.exp(local_peak - global_peak), 'dp')  236 us
    all_gather x1, waiting for transfers between devices, shards(): right_all = lax.all_gather(right_bf, 'dp', axis=0, tiled=True)  129 us
    psum x1, blocking collectives, shards(): lax.psum(jnp.sum(row_lse + column_own - 2.0 * matched), 'dp')  76.3 us
    pmax x1, blocking collectives, shards(): lax.pmax(local_peak.astype(jnp.bfloat16), 'dp').astype(local_peak.dtype)  74.7 us
    all_gather x1, waiting for transfers between devices, shards(): shard_rows = lax.all_gather(left_bf, 'dp', axis=0, tiled=True)  35.7 us
    dot_general x1, matrix products, shards(): lax.dot_general(part_bf, shard_rows, (((0,), (0,)), ((), ())), preferred_...  17.8 us
    dot_general x1, matrix products, shards(): lax.dot_general(left_bf, right_all, (((1,), (1,)), ((), ())), preferred_e...  13.2 us
  transfers between devices with their start and end apart: 3, of which 3 were waited for; matrix products, arithmetic and copies ran while one was open for 2% of the time, Pallas kernels for 0%

commit v1 on v0

v1 whole, which is shorter than its diff:
```python
import functools
import math

import jax
import jax.numpy as jnp
from jax import lax
from jax.experimental import pallas as pl
from jax.experimental.pallas import tpu as pltpu
from jax.sharding import PartitionSpec as P

MESH = pl.DeviceIdType.MESH
G = 16
ROWS = 72
D = 384
B = G * ROWS
TM = 288
T = B // TM
PER = TM // ROWS
LOG2E = math.log2(math.e)
LN2 = math.log(2.0)


def kernel(
    left_ref, right_ref, lgrad_ref, rgrad_ref, loss_ref,
    lg, rg, lall, rall, er, ec, w, rm_s, rl_s, cm_s, cs_s, rp,
    row_stat, col_stat, ls, rs, lr, rr, part, parts_a, parts_b,
    s_lg, r_lg, s_rg, r_rg, s_st, r_st, s_ls, r_ls, s_rs, r_rs, s_pa, r_pa, s_pb, r_pb,
):
    me = lax.axis_index("dp")
    core = me % 2
    p = (me // 2) % G
    z = me // (2 * G)
    q = z * 2 + core
    scale = 2.0 / math.sqrt(D) * LOG2E

    def plane_dev(k):
        return (z * (2 * G) + k * 2 + core,)

    def line_dev(k):
        return ((k // 2) * (2 * G) + p * 2 + k % 2,)

    barrier = pltpu.get_barrier_semaphore()

    @pl.loop(1, G)
    def _(m):
        pl.semaphore_signal(barrier, inc=1, device_id=plane_dev((p + m) % G), device_id_type=MESH)
        pl.semaphore_signal(barrier, inc=1, device_id=line_dev((q + m) % G), device_id_type=MESH)

    lbf = left_ref[...].astype(jnp.bfloat16)
    rbf = right_ref[...].astype(jnp.bfloat16)
    lg[p] = lbf
    rg[q] = rbf
    matched = jnp.sum(lbf.astype(jnp.float32) * rbf.astype(jnp.float32)) * scale
    pl.semaphore_wait(barrier, 2 * (G - 1))

    def copy(src, dst, send, recv, dev):
        return pltpu.make_async_remote_copy(
            src_ref=src, dst_ref=dst, send_sem=send, recv_sem=recv, device_id=dev, device_id_type=MESH
        )

    @pl.loop(1, G)
    def _(m):
        k = (p + m) % G
        copy(lg.at[p], lg.at[p], s_lg.at[k], r_lg.at[p], plane_dev(k)).start()
        k = (q + m) % G
        copy(rg.at[q], rg.at[q], s_rg.at[k], r_rg.at[q], line_dev(k)).start()

    @pl.loop(1, G)
    def _(m):
        k = (p + m) % G
        copy(lg.at[p], lg.at[k], s_lg.at[k], r_lg.at[k], plane_dev(k)).wait()
        k = (q + m) % G
        copy(rg.at[q], rg.at[k], s_rg.at[k], r_rg.at[k], line_dev(k)).wait()

    @pl.loop(0, G // 2)
    def _(j):
        at = pl.ds(pl.multiple_of(j * 2 * ROWS, 2 * ROWS), 2 * ROWS)
        for src, dst in ((lg, lall), (rg, rall)):
            two = [src[2 * j].astype(jnp.float32), src[2 * j + 1].astype(jnp.float32)]
            dst[at, :] = jnp.concatenate(two, axis=0).astype(jnp.bfloat16)

    @pl.loop(0, T)
    def _(t):
        at = pl.ds(pl.multiple_of(t * TM, TM), TM)
        s = lax.dot_general(
            lall[at, :], rall[...], (((1,), (1,)), ((), ())), preferred_element_type=jnp.float32
        ) * scale
        rm = jnp.max(s, axis=1, keepdims=True)
        e = jnp.exp2(s - rm)
        er[at, :] = e
        rm_s[at, :] = jnp.broadcast_to(rm, (TM, 128))
        rl_s[at, :] = jnp.broadcast_to(rm + jnp.log2(jnp.sum(e, axis=1, keepdims=True)), (TM, 128))
        cm = jnp.max(s, axis=0, keepdims=True)
        e = jnp.exp2(s - cm)
        ec[at, :] = e
        cm_s[t] = cm
        cs_s[t] = jnp.sum(e, axis=0, keepdims=True)

    cm = jnp.max(cm_s[...], axis=0)
    cs = jnp.sum(cs_s[...] * jnp.exp2(cm_s[...] - cm[None]), axis=0)
    col_stat[q] = cm + jnp.log2(cs)
    row_stat[p] = jnp.transpose(rl_s[...])[0:1, :]

    @pl.loop(1, G)
    def _(m):
        k = (p + m) % G
        copy(row_stat.at[p], row_stat.at[p], s_st.at[k], r_st.at[p], plane_dev(k)).start()
        k = (q + m) % G
        copy(col_stat.at[q], col_stat.at[q], s_st.at[G + k], r_st.at[G + q], line_dev(k)).start()

    @pl.loop(1, G)
    def _(m):
        k = (p + m) % G
        copy(row_stat.at[p], row_stat.at[k], s_st.at[k], r_st.at[k], plane_dev(k)).wait()
        k = (q + m) % G
        copy(col_stat.at[q], col_stat.at[k], s_st.at[G + k], r_st.at[G + k], line_dev(k)).wait()

    def combine(ref):
        v = ref[...]
        top = jnp.max(v, axis=0)
        return top + jnp.log2(jnp.sum(jnp.exp2(v - top[None]), axis=0))

    row_lse = combine(row_stat)
    col_lse = combine(col_stat)
    row_lse_col = jnp.transpose(jnp.broadcast_to(row_lse, (128, B)))
    rm_s[...] = jnp.exp2(rm_s[...] - row_lse_col)

    lane = lax.broadcasted_iota(jnp.int32, (1, B), 1)
    own = (lane >= p * ROWS) & (lane < (p + 1) * ROWS)
    mine_row = jnp.sum(jnp.where(own, row_lse, 0.0)) - 2.0 * matched
    part[...] = jnp.full((1, 128), mine_row, jnp.float32)
    own_c = (lane >= q * ROWS) & (lane < (q + 1) * ROWS)
    mine = mine_row + jnp.sum(jnp.where(own_c, col_lse, 0.0))
    parts_a[p] = jnp.full((1, 128), mine, jnp.float32)

    @pl.loop(1, G)
    def _(m):
        k = (p + m) % G
        copy(parts_a.at[p], parts_a.at[p], s_pa.at[k], r_pa.at[p], plane_dev(k)).start()

    col_loc = lax.broadcasted_iota(jnp.int32, (1, B), 1) - q * ROWS
    col_loc = jnp.where((col_loc >= 0) & (col_loc < ROWS), col_loc, -2)

    @pl.loop(0, T)
    def _(t):
        at = pl.ds(pl.multiple_of(t * TM, TM), TM)
        fr = rm_s[at, 0:1]
        fc = jnp.exp2(cm_s[t] - col_lse)
        row_loc = lax.broadcasted_iota(jnp.int32, (TM, 1), 0) + (t * TM - p * ROWS)
        row_loc = jnp.where((row_loc >= 0) & (row_loc < ROWS), row_loc, -1)
        ww = er[at, :] * fr + ec[at, :] * fc
        ww = jnp.where(row_loc == col_loc, ww - 2.0, ww)
        wb = ww.astype(jnp.bfloat16)
        w[at, :] = wb
        lp = jnp.dot(wb, rall[...], preferred_element_type=jnp.float32)
        for j in range(PER):
            k = t * PER + j
            ls[k] = lp[j * ROWS : (j + 1) * ROWS, :].astype(jnp.bfloat16)

            @pl.when(k != p)
            def _():
                copy(ls.at[k], lr.at[p], s_ls.at[k], r_ls.at[p], plane_dev(k)).start()

            @pl.when(k == p)
            def _():
                lgrad_ref[...] = lp[j * ROWS : (j + 1) * ROWS, :]

    @pl.loop(0, 3)
    def _(u):
        at = pl.ds(pl.multiple_of(u * 384, 384), 384)
        rp[at, :] = lax.dot_general(
            w[:, at], lall[...], (((0,), (0,)), ((), ())), preferred_element_type=jnp.float32
        )

    @pl.loop(0, G)
    def _(k):
        piece = rp[pl.ds(pl.multiple_of(k * ROWS, ROWS), ROWS), :]
        rs[k] = piece.astype(jnp.bfloat16)

        @pl.when(k != q)
        def _():
            copy(rs.at[k], rr.at[q], s_rs.at[k], r_rs.at[q], line_dev(k)).start()

        @pl.when(k == q)
        def _():
            rgrad_ref[...] = piece

    @pl.loop(1, G)
    def _(m):
        k = (p + m) % G
        copy(parts_a.at[p], parts_a.at[k], s_pa.at[k], r_pa.at[k], plane_dev(k)).wait()

    parts_b[q] = jnp.sum(parts_a[...], axis=0)

    @pl.loop(1, G)
    def _(m):
        k = (q + m) % G
        copy(parts_b.at[q], parts_b.at[q], s_pb.at[k], r_pb.at[q], line_dev(k)).start()

    @pl.loop(1, G)
    def _(m):
        k = (p + m) % G
        copy(ls.at[k], lr.at[k], s_ls.at[k], r_ls.at[k], plane_dev(k)).wait()
        lgrad_ref[...] += lr[k].astype(jnp.float32)

    @pl.loop(1, G)
    def _(m):
        k = (q + m) % G
        copy(rs.at[k], rr.at[k], s_rs.at[k], r_rs.at[k], line_dev(k)).wait()
        rgrad_ref[...] += rr[k].astype(jnp.float32)

    @pl.loop(1, G)
    def _(m):
        k = (q + m) % G
        copy(parts_b.at[q], parts_b.at[k], s_pb.at[k], r_pb.at[k], line_dev(k)).wait()

    loss_ref[...] = jnp.sum(parts_b[...], axis=0) * (LN2 / (2.0 * G * G * ROWS))


def shards(left, right):
    f32, bf16 = jnp.float32, jnp.bfloat16
    vmem = pl.BlockSpec(memory_space=pltpu.VMEM)
    dma = pltpu.SemaphoreType.DMA
    left_grad, right_grad, loss = pl.pallas_call(
        kernel,
        out_shape=(
            jax.ShapeDtypeStruct((ROWS, D), f32),
            jax.ShapeDtypeStruct((ROWS, D), f32),
            jax.ShapeDtypeStruct((1, 128), f32),
        ),
        in_specs=[vmem, vmem],
        out_specs=(vmem, vmem, vmem),
        scratch_shapes=[
            pltpu.VMEM((G, ROWS, D), bf16),
            pltpu.VMEM((G, ROWS, D), bf16),
            pltpu.VMEM((B, D), bf16),
            pltpu.VMEM((B, D), bf16),
            pltpu.VMEM((B, B), f32),
            pltpu.VMEM((B, B), f32),
            pltpu.VMEM((B, B), bf16),
            pltpu.VMEM((B, 128), f32),
            pltpu.VMEM((B, 128), f32),
            pltpu.VMEM((T, 1, B), f32),
            pltpu.VMEM((T, 1, B), f32),
            pltpu.VMEM((B, D), f32),
            pltpu.VMEM((G, 1, B), f32),
            pltpu.VMEM((G, 1, B), f32),
            pltpu.VMEM((G, ROWS, D), bf16),
            pltpu.VMEM((G, ROWS, D), bf16),
            pltpu.VMEM((G, ROWS, D), bf16),
            pltpu.VMEM((G, ROWS, D), bf16),
            pltpu.VMEM((1, 128), f32),
            pltpu.VMEM((G, 1, 128), f32),
            pltpu.VMEM((G, 1, 128), f32),
            dma((G,)), dma((G,)), dma((G,)), dma((G,)),
            dma((2 * G,)), dma((2 * G,)),
            dma((G,)), dma((G,)), dma((G,)), dma((G,)),
            dma((G,)), dma((G,)), dma((G,)), dma((G,)),
        ],
        compiler_params=pltpu.CompilerParams(
            collective_id=0, has_side_effects=True, vmem_limit_bytes=56 * 2**20
        ),
        cost_estimate=pl.CostEstimate(flops=6 * B * B * D, bytes_accessed=4 * ROWS * D * 4, transcendentals=2 * B * B),
        name="infonce",
    )(left, right)
    return left_grad, right_grad, loss[0, 0]


def solution(mesh):
    return jax.shard_map(
        shards,
        mesh=mesh,
        in_specs=(P("dp", None), P("dp", None)),
        out_specs=(P("dp", None), P("dp", None), P()),
        check_vma=False,
    )
```

time: 622 us -> 77.1 us (0.12)
  waiting for transfers between devices: 401 us -> 0 us
  blocking collectives: 151 us -> 0 us
  Pallas kernels: 0 us -> 72.9 us
  matrix products: 41.2 us -> 0 us
  between operations: 15.6 us -> 1.81 us
  other arithmetic: 9.07 us -> 0 us
    psum x1 -> x0, waiting for transfers between devices: 236 us -> none  [shards(): global_mass = lax.psum(local_mass * jnp.exp(local_peak - global_peak), 'dp')]
    all_gather x2 -> x0, waiting for transfers between devices: 165 us -> none  [the longest x1 129 us: shards(): right_all = lax.all_gather(right_bf, 'dp', axis=0, tiled=True)]
    psum x1 -> x0, blocking collectives: 76.3 us -> none  [shards(): lax.psum(jnp.sum(row_lse + column_own - 2.0 * matched), 'dp')]
    pmax x1 -> x0, blocking collectives: 74.7 us -> none  [shards(): lax.pmax(local_peak.astype(jnp.bfloat16), 'dp').astype(local_peak.dtype)]
    pallas_call x0 -> x1, Pallas kernels: none -> 72.9 us  [shards(): pl.pallas_call(kernel, out_shape=(jax.ShapeDtypeStruct((ROWS, D), f32), j...]
    dot_general x3 -> x0, matrix products: 41.2 us -> none  [the longest x1 17.8 us: shards(): lax.dot_general(part_bf, shard_rows, (((0,), (0,)), ((), ())), preferred_...]
  transfers between devices with their start and end apart: 3 -> 0, of which waited for: 3 -> 0; matrix products, arithmetic and copies ran while one was open for 2% -> 0% of each run, Pallas kernels for 0% -> 0%
where the time goes in v1:
time: 77.1 us; the launch traced here: 77 us
  Pallas kernels  72.9 us (95%)
  local copies, waits for them, and re-layouts  2.24 us (3%)
  between operations  1.81 us (2%)
    pallas_call x1, Pallas kernels, shards(): pl.pallas_call(kernel, out_shape=(jax.ShapeDtypeStruct((ROWS, D), f32), j...  72.9 us
    unnamed x6, local copies, waits for them, and re-layouts  2.24 us

profile of v1, /device:TPU:1, one launch (start us, length us, event | category | flops | bytes accessed | tf_op | source)
XLA Modules:
  0.0 77.0 jit_solution(8468452356589956212)
XLA Ops:
  0.6 72.9 %infonce.1 = (f32[72,384]{1,0:T(8,128)}, f32[72,384]{1,0:T(8,128)}, f32[1,128]{1,0:T(1,128)}) custom-call(f32[72,384]{1,0:T(8,128)} %left_ref.1, f32[72,384]{1,0:T(8,128)} %right_ref.1), custom_call_target="tpu_custom_call" | custom-call | flops 3057647616 | bytes 442368 | tf_op jit(solution)/shard_map/infonce/pallas_call | solution.py:224
  73.5 0.0 copy-start
  73.5 1.6 %copy.8 = f32[72,384]{1,0:T(8,128)} copy(f32[72,384]{1,0:T(8,128)} %get-tuple-element.12) | data formatting | bytes 221184
  75.1 0.0 copy-done
  75.1 0.0 copy-start.1
  75.1 0.6 copy.9
  75.8 0.0 copy-done.1
Async XLA Ops:
  73.5 1.6 %copy-start = (f32[72,384]{1,0:T(8,128)S(1)}, f32[72,384]{1,0:T(8,128)}, u32[]{:S(2)}) copy-start(f32[72,384]{1,0:T(8,128)} %get-tuple-element.13) | copy-start | bytes 331780
  75.1 0.6 copy-start.1

commit v2 on v0

v2 whole, which is shorter than its diff:
```python
import math

import jax
import jax.numpy as jnp
from jax import lax
from jax.experimental import pallas as pl
from jax.experimental.pallas import tpu as pltpu
from jax.sharding import PartitionSpec as P

MESH = pl.DeviceIdType.MESH
NZ = 8
NA = 4
G = 16
ROWS = 72
D = 384
B = G * ROWS
TM = 4 * ROWS
CHUNKS = B // TM
TN = 384
LOG2E = math.log2(math.e)
LN2 = math.log(2.0)

A_OFFS = (2, 1, 3)
PLANE_OFFS = sorted(
    [(i, j) for i in range(NA) for j in range(NA) if (i, j) != (0, 0)],
    key=lambda o: -(min(o[0], NA - o[0]) + min(o[1], NA - o[1])),
)
LINE_OFFS = sorted(
    [(i, j) for i in range(NZ) for j in range(2) if (i, j) != (0, 0)],
    key=lambda o: -min(o[0], NZ - o[0]),
)


def kernel(
    left_ref, right_ref, lgrad_ref, rgrad_ref, loss_ref,
    lin, rin, lg, rg, lall, rall, er, ec, w, rm_s, rl_s, cm_s, cs_s, rp, ap,
    row_stat, col_stat, bs, br, sib_s, sib_r, zs, zr, zm, part_a, part_b,
    s_in, s_l, r_l, s_sib, r_sib, s_r, r_r, s_f, s_row, r_row, s_col, r_col,
    s_gb, r_gb, s_gs, r_gs, s_gz, r_gz, r_gm, s_pa, r_pa, s_pb, r_pb,
):
    me = lax.axis_index("dp")
    core = me % 2
    x = (me // 2) % NA
    y = (me // (2 * NA)) % NA
    z = me // (2 * G)
    a = y * (1 - core) + x * core
    b = x * (1 - core) + y * core
    step_a = 8 - 6 * core
    step_b = 2 + 6 * core
    p = a * NA + b
    q = z * 2 + core
    other = 1 - core
    sg = 1 - 2 * core
    scale = 2.0 / math.sqrt(D) * LOG2E

    def plane_dev(pa, pb):
        return (z * (2 * G) + pa * step_a + pb * step_b + core,)

    def line_dev(pz, pc):
        return (pz * (2 * G) + (y * NA + x) * 2 + pc,)

    def zz(d):
        return (z + d + NZ) % NZ

    sends = []

    def copy(src, dst, send, recv, dev):
        return pltpu.make_async_remote_copy(
            src_ref=src, dst_ref=dst, send_sem=send, recv_sem=recv, device_id=dev, device_id_type=MESH
        )

    def go(src, dst, send, recv, dev):
        c = copy(src, dst, send, recv, dev)
        c.start()
        sends.append(c)

    c_left = pltpu.make_async_copy(left_ref, lin, s_in.at[0])
    c_right = pltpu.make_async_copy(right_ref, rin, s_in.at[1])
    c_left.start()
    c_right.start()
    barrier = pltpu.get_barrier_semaphore()
    for i in range(G - 1):
        da, db = PLANE_OFFS[i]
        dev = plane_dev((a + da) % NA, (b + db) % NA)
        pl.semaphore_signal(barrier, inc=1, device_id=dev, device_id_type=MESH)
        dz, dc = LINE_OFFS[i]
        dev = line_dev((z + dz) % NZ, (core + dc) % 2)
        pl.semaphore_signal(barrier, inc=1, device_id=dev, device_id_type=MESH)
    c_left.wait()
    c_right.wait()
    lbf = lin[...].astype(jnp.bfloat16)
    rbf = rin[...].astype(jnp.bfloat16)
    lg[q] = lbf
    rg[p] = rbf
    matched = jnp.sum(lbf.astype(jnp.float32) * rbf.astype(jnp.float32)) * scale
    pl.semaphore_wait(barrier, 2 * (G - 1))

    def line_slot(k, c):
        return lg.at[k * 2 + c]

    def line_wait(d):
        k = zz(d)
        copy(lg.at[q], line_slot(k, core), s_l.at[0], r_l.at[k], line_dev(k, core)).wait_recv()
        return k

    def to_sibling(k):
        piece = line_slot(k, core)
        go(piece, piece, s_sib.at[k], r_sib.at[k], line_dev(z, other))

    def relay(k, i, d):
        piece = line_slot(k, core)
        go(piece, piece, s_l.at[i], r_l.at[k], line_dev(zz(d), core))

    def plane_wait(ka, kb):
        k = ka * NA + kb
        copy(rg.at[p], rg.at[k], s_r.at[0], r_r.at[k], plane_dev(ka, kb)).wait_recv()
        return k

    for i, d in enumerate((2, -2, 1, -1)):
        go(lg.at[q], lg.at[q], s_l.at[i], r_l.at[z], line_dev(zz(d), core))
    for i, d in enumerate(A_OFFS):
        go(rg.at[p], rg.at[p], s_r.at[i], r_r.at[p], plane_dev(a, (b + d) % NA))
    for i, d in enumerate(A_OFFS):
        go(rg.at[p], rg.at[p], s_r.at[3 + i], r_r.at[p], plane_dev((a + d) % NA, b))
    to_sibling(z)
    for n, db in enumerate((1, 3, 2)):
        k = plane_wait(a, (b + db) % NA)
        for i, d in enumerate(A_OFFS):
            go(rg.at[k], rg.at[k], s_f.at[n * 3 + i], r_r.at[k], plane_dev((a + d) % NA, b))
    k = line_wait(-2 * sg)
    relay(k, 4, 2 * sg)
    relay(k, 5, sg)
    k2 = line_wait(2 * sg)
    relay(k2, 6, -sg)
    to_sibling(k)
    to_sibling(k2)
    for d in (1, -1, 3 * sg, -3 * sg, 4):
        to_sibling(line_wait(d))
    for da in (1, 3, 2):
        for db in (0, 1, 3, 2):
            plane_wait((a + da) % NA, (b + db) % NA)

    def join(src, k, dst, at):
        two = [src[k].astype(jnp.float32), src[k + 1].astype(jnp.float32)]
        dst[pl.ds(pl.multiple_of(at, 2 * ROWS), 2 * ROWS), :] = jnp.concatenate(two, axis=0).astype(jnp.bfloat16)

    @pl.loop(0, G // 2)
    def _(j):
        join(rg, 2 * j, rall, j * 2 * ROWS)

    zp = z // 2
    near = 1 - 2 * (z % 2)

    def scores(t):
        for j in range(2):
            k = 2 * t + j
            copy(lg.at[q], line_slot(k, other), s_sib.at[0], r_sib.at[k], line_dev(z, other)).wait_recv()
            join(lg, 2 * k, lall, k * 2 * ROWS)
        at = pl.ds(pl.multiple_of(t * TM, TM), TM)
        s = lax.dot_general(
            lall[at, :], rall[...], (((1,), (1,)), ((), ())), preferred_element_type=jnp.float32
        ) * scale
        rm = jnp.max(s, axis=1, keepdims=True)
        e = jnp.exp2(s - rm)
        er[at, :] = e
        rm_s[at, :] = jnp.broadcast_to(rm, (TM, 128))
        rl_s[at, :] = jnp.broadcast_to(rm + jnp.log2(jnp.sum(e, axis=1, keepdims=True)), (TM, 128))
        cm = jnp.max(s, axis=0, keepdims=True)
        e = jnp.exp2(s - cm)
        ec[at, :] = e
        cm_s[t] = cm
        cs_s[t] = jnp.sum(e, axis=0, keepdims=True)

    @pl.loop(0, CHUNKS)
    def _(o):
        shift = (o % 2) * (1 - o // 2) * near - (o // 2) * (1 - o % 2) * near + (o // 2) * (o % 2) * 2
        scores((zp + shift + CHUNKS) % CHUNKS)

    cm = jnp.max(cm_s[...], axis=0)
    cs = jnp.sum(cs_s[...] * jnp.exp2(cm_s[...] - cm[None]), axis=0)
    col_stat[p, :, 0:B] = cm + jnp.log2(cs)
    col_stat[p, :, B : B + 128] = jnp.full((1, 128), matched, jnp.float32)
    row_stat[q] = jnp.transpose(rl_s[...])[0:1, :]

    for i in range(G - 1):
        dz, dc = LINE_OFFS[i]
        dev = line_dev((z + dz) % NZ, (core + dc) % 2)
        go(row_stat.at[q], row_stat.at[q], s_row.at[i], r_row.at[q], dev)
        da, db = PLANE_OFFS[i]
        dev = plane_dev((a + da) % NA, (b + db) % NA)
        go(col_stat.at[p], col_stat.at[p], s_col.at[i], r_col.at[p], dev)
    for i in range(G - 1):
        dz, dc = LINE_OFFS[-1 - i]
        kz, kc = (z + dz) % NZ, (core + dc) % 2
        k = kz * 2 + kc
        copy(row_stat.at[q], row_stat.at[k], s_row.at[i], r_row.at[k], line_dev(kz, kc)).wait_recv()
        da, db = PLANE_OFFS[-1 - i]
        ka, kb = (a + da) % NA, (b + db) % NA
        k = ka * NA + kb
        copy(col_stat.at[p], col_stat.at[k], s_col.at[i], r_col.at[k], plane_dev(ka, kb)).wait_recv()

    def combine(v):
        top = jnp.max(v, axis=0)
        return top + jnp.log2(jnp.sum(jnp.exp2(v - top[None]), axis=0))

    row_lse = combine(row_stat[...])
    col_lse = combine(col_stat[:, :, 0:B])
    rm_s[...] = jnp.exp2(rm_s[...] - jnp.transpose(jnp.broadcast_to(row_lse, (128, B))))

    pairs = jnp.sum(col_stat[:, :, B : B + 128], axis=0)
    part_a[q] = jnp.sum(col_lse) - 2.0 * pairs
    part_b[p] = jnp.full((1, 128), jnp.sum(row_lse), jnp.float32)

    col_loc = lax.broadcasted_iota(jnp.int32, (1, B), 1) - p * ROWS
    col_loc = jnp.where((col_loc >= 0) & (col_loc < ROWS), col_loc, -2)

    @pl.loop(0, CHUNKS)
    def _(t):
        at = pl.ds(pl.multiple_of(t * TM, TM), TM)
        fc = jnp.exp2(cm_s[t] - col_lse)
        row_loc = lax.broadcasted_iota(jnp.int32, (TM, 1), 0) + (t * TM - q * ROWS)
        row_loc = jnp.where((row_loc >= 0) & (row_loc < ROWS), row_loc, -1)
        ww = er[at, :] * rm_s[at, 0:1] + ec[at, :] * fc
        w[at, :] = jnp.where(row_loc == col_loc, ww - 2.0, ww).astype(jnp.bfloat16)

    first = 0
    for u in range(B // TN):
        rp[u * TN : (u + 1) * TN, :] = lax.dot_general(
            w[:, u * TN : (u + 1) * TN], lall[...], (((0,), (0,)), ((), ())), preferred_element_type=jnp.float32
        )
        last = (u + 1) * TN // ROWS

        @pl.loop(first, last)
        def _(k):
            piece = rp[pl.ds(pl.multiple_of(k * ROWS, ROWS), ROWS), :]
            bs[k] = piece.astype(jnp.bfloat16)

            @pl.when(k != p)
            def _():
                copy(bs.at[k], br.at[p], s_gb.at[k], r_gb.at[p], plane_dev(k // NA, k % NA)).start()

            @pl.when(k == p)
            def _():
                rgrad_ref[...] = piece

        first = last

    @pl.loop(0, CHUNKS)
    def _(o):
        back = 3 - o
        shift = (back % 2) * (1 - back // 2) * near - (back // 2) * (1 - back % 2) * near + (back // 2) * (back % 2) * 2
        t = (zp + shift + CHUNKS) % CHUNKS
        at = pl.ds(pl.multiple_of(t * TM, TM), TM)
        part = jnp.dot(w[at, :], rall[...], preferred_element_type=jnp.float32)
        for j in range(2):
            k = 2 * t + j
            lo = part[2 * j * ROWS : (2 * j + 1) * ROWS, :]
            hi = part[(2 * j + 1) * ROWS : (2 * j + 2) * ROWS, :]
            mine = jnp.where(core == 0, lo, hi)
            yours = jnp.where(core == 0, hi, lo)
            ap[k] = mine
            sib_s[k] = yours.astype(jnp.bfloat16)
            copy(sib_s.at[k], sib_r.at[k], s_gs.at[k], r_gs.at[k], line_dev(z, other)).start()

    def chip_sum(k):
        copy(sib_s.at[k], sib_r.at[k], s_gs.at[k], r_gs.at[k], line_dev(z, other)).wait_recv()
        return ap[k] + sib_r[k].astype(jnp.float32)

    def mid(i, owner, d):
        zs[i] = chip_sum(zz(owner)).astype(jnp.bfloat16)
        go(zs.at[i], zm.at[i], s_gz.at[i], r_gm.at[i], line_dev(zz(d), core))

    def mid_wait(i):
        copy(zs.at[i], zm.at[i], s_gz.at[i], r_gm.at[i], line_dev(z, other)).wait_recv()
        return zm[i].astype(jnp.float32)

    def end(i, d, value):
        zs[i] = value.astype(jnp.bfloat16)
        go(zs.at[i], zr.at[i - 3], s_gz.at[i], r_gz.at[i - 3], line_dev(zz(d), core))

    mid(0, 4, -2 * sg)
    mid(1, -3 * sg, -sg)
    mid(2, 3 * sg, sg)
    end(3, 1, chip_sum(zz(1)))
    end(4, -1, chip_sum(zz(-1)))
    plus = chip_sum(zz(2 * sg))
    minus = chip_sum(zz(-2 * sg))
    lgrad_ref[...] = chip_sum(z)
    end(5, 2 * sg, plus + mid_wait(2))
    end(6, -2 * sg, minus + mid_wait(0) + mid_wait(1))

    for i in range(G - 1):
        da, db = PLANE_OFFS[i]
        dev = plane_dev((a + da) % NA, (b + db) % NA)
        go(part_b.at[p], part_b.at[p], s_pb.at[i], r_pb.at[p], dev)
        dz, dc = LINE_OFFS[i]
        dev = line_dev((z + dz) % NZ, (core + dc) % 2)
        go(part_a.at[q], part_a.at[q], s_pa.at[i], r_pa.at[q], dev)
    for da, db in reversed(PLANE_OFFS):
        ka, kb = (a + da) % NA, (b + db) % NA
        k = ka * NA + kb
        copy(bs.at[k], br.at[k], s_gb.at[k], r_gb.at[k], plane_dev(ka, kb)).wait()
        rgrad_ref[...] += br[k].astype(jnp.float32)
    for i in range(G - 1):
        da, db = PLANE_OFFS[i]
        ka, kb = (a + da) % NA, (b + db) % NA
        k = ka * NA + kb
        copy(part_b.at[p], part_b.at[k], s_pb.at[i], r_pb.at[k], plane_dev(ka, kb)).wait_recv()
        dz, dc = LINE_OFFS[i]
        kz, kc = (z + dz) % NZ, (core + dc) % 2
        k = kz * 2 + kc
        copy(part_a.at[q], part_a.at[k], s_pa.at[i], r_pa.at[k], line_dev(kz, kc)).wait_recv()
    loss_ref[...] = (jnp.sum(part_a[...], axis=0) + jnp.sum(part_b[...], axis=0)) * (LN2 / (2.0 * NZ * 2 * B))
    for i in range(4):
        copy(zs.at[3 + i], zr.at[i], s_gz.at[i], r_gz.at[i], line_dev(z, other)).wait_recv()
        lgrad_ref[...] += zr[i].astype(jnp.float32)
    for k in range(NZ):
        copy(sib_s.at[k], sib_r.at[k], s_gs.at[k], r_gs.at[k], line_dev(z, other)).wait_send()
    for c in sends:
        c.wait_send()


def shards(left, right):
    f32, bf16 = jnp.float32, jnp.bfloat16
    anywhere = pl.BlockSpec(memory_space=pl.ANY)
    vmem = pl.BlockSpec(memory_space=pltpu.VMEM)
    dma = pltpu.SemaphoreType.DMA
    left_grad, right_grad, loss = pl.pallas_call(
        kernel,
        out_shape=(pltpu.VMEM((ROWS, D), f32), pltpu.VMEM((ROWS, D), f32), pltpu.VMEM((1, 128), f32)),
        in_specs=[anywhere, anywhere],
        out_specs=(vmem, vmem, vmem),
        scratch_shapes=[
            pltpu.VMEM((ROWS, D), f32),
            pltpu.VMEM((ROWS, D), f32),
            pltpu.VMEM((G, ROWS, D), bf16),
            pltpu.VMEM((G, ROWS, D), bf16),
            pltpu.VMEM((B, D), bf16),
            pltpu.VMEM((B, D), bf16),
            pltpu.VMEM((B, B), f32),
            pltpu.VMEM((B, B), f32),
            pltpu.VMEM((B, B), bf16),
            pltpu.VMEM((B, 128), f32),
            pltpu.VMEM((B, 128), f32),
            pltpu.VMEM((CHUNKS, 1, B), f32),
            pltpu.VMEM((CHUNKS, 1, B), f32),
            pltpu.VMEM((B, D), f32),
            pltpu.VMEM((NZ, ROWS, D), f32),
            pltpu.VMEM((G, 1, B), f32),
            pltpu.VMEM((G, 1, B + 128), f32),
            pltpu.VMEM((G, ROWS, D), bf16),
            pltpu.VMEM((G, ROWS, D), bf16),
            pltpu.VMEM((NZ, ROWS, D), bf16),
            pltpu.VMEM((NZ, ROWS, D), bf16),
            pltpu.VMEM((7, ROWS, D), bf16),
            pltpu.VMEM((4, ROWS, D), bf16),
            pltpu.VMEM((3, ROWS, D), bf16),
            pltpu.VMEM((G, 1, 128), f32),
            pltpu.VMEM((G, 1, 128), f32),
            dma((2,)),
            dma((NZ,)), dma((NZ,)),
            dma((NZ,)), dma((NZ,)),
            dma((6,)), dma((G,)),
            dma((9,)),
            dma((G,)), dma((G,)),
            dma((G,)), dma((G,)),
            dma((G,)), dma((G,)),
            dma((NZ,)), dma((NZ,)),
            dma((7,)), dma((4,)), dma((3,)),
            dma((G,)), dma((G,)),
            dma((G,)), dma((G,)),
        ],
        compiler_params=pltpu.CompilerParams(
            collective_id=0, has_side_effects=True, vmem_limit_bytes=56 * 2**20
        ),
        cost_estimate=pl.CostEstimate(flops=6 * B * B * D, bytes_accessed=16 * ROWS * D, transcendentals=2 * B * B),
        name="infonce",
    )(left, right)
    return left_grad, right_grad, loss[0, 0]


def solution(mesh):
    return jax.shard_map(
        shards,
        mesh=mesh,
        in_specs=(P("dp", None), P("dp", None)),
        out_specs=(P("dp", None), P("dp", None), P()),
        check_vma=False,
    )
```

time: 622 us -> 54.3 us (0.09)
  waiting for transfers between devices: 401 us -> 0 us
  blocking collectives: 151 us -> 0 us
  Pallas kernels: 0 us -> 51.1 us
  matrix products: 41.2 us -> 0 us
  between operations: 15.6 us -> 1.8 us
  other arithmetic: 9.07 us -> 0 us
    psum x1 -> x0, waiting for transfers between devices: 236 us -> none  [shards(): global_mass = lax.psum(local_mass * jnp.exp(local_peak - global_peak), 'dp')]
    all_gather x2 -> x0, waiting for transfers between devices: 165 us -> none  [the longest x1 129 us: shards(): right_all = lax.all_gather(right_bf, 'dp', axis=0, tiled=True)]
    psum x1 -> x0, blocking collectives: 76.3 us -> none  [shards(): lax.psum(jnp.sum(row_lse + column_own - 2.0 * matched), 'dp')]
    pmax x1 -> x0, blocking collectives: 74.7 us -> none  [shards(): lax.pmax(local_peak.astype(jnp.bfloat16), 'dp').astype(local_peak.dtype)]
    pallas_call x0 -> x1, Pallas kernels: none -> 51.1 us  [shards(): pl.pallas_call(kernel, out_shape=(pltpu.VMEM((ROWS, D), f32), pltpu.VMEM(...]
    dot_general x3 -> x0, matrix products: 41.2 us -> none  [the longest x1 17.8 us: shards(): lax.dot_general(part_bf, shard_rows, (((0,), (0,)), ((), ())), preferred_...]
  transfers between devices with their start and end apart: 3 -> 0, of which waited for: 3 -> 0; matrix products, arithmetic and copies ran while one was open for 2% -> 0% of each run, Pallas kernels for 0% -> 0%
where the time goes in v2:
time: 54.3 us; the launch traced here: 54.1 us
  Pallas kernels  51.1 us (94%)
  between operations  1.8 us (3%)
  local copies, waits for them, and re-layouts  1.29 us (2%)
    pallas_call x1, Pallas kernels, shards(): pl.pallas_call(kernel, out_shape=(pltpu.VMEM((ROWS, D), f32), pltpu.VMEM(...  51.1 us
    unnamed x2, local copies, waits for them, and re-layouts  1.29 us

profile of v2, /device:TPU:1, one launch (start us, length us, event | category | flops | bytes accessed | tf_op | source)
XLA Modules:
  0.0 54.1 jit_solution(148935125136444603)
XLA Ops:
  0.6 51.1 %infonce.1 = (f32[72,384]{1,0:T(8,128)S(1)}, f32[72,384]{1,0:T(8,128)S(1)}, f32[1,128]{1,0:T(1,128)S(1)}) custom-call(f32[72,384]{1,0:T(8,128)} %left_ref.1, f32[72,384]{1,0:T(8,128)} %right_ref.1), custom_call_target="tpu_custom_call" | custom-call | flops 3057647616 | bytes 442368 | tf_op jit(solution)/shard_map/infonce/pallas_call | solution.py:328
  51.7 0.6 %copy.8 = f32[72,384]{1,0:T(8,128)} copy(f32[72,384]{1,0:T(8,128)S(1)} %get-tuple-element.9) | data formatting | bytes 221184
  52.3 0.6 %copy.9 = f32[72,384]{1,0:T(8,128)} copy(f32[72,384]{1,0:T(8,128)S(1)} %get-tuple-element.10) | data formatting | bytes 221184

commit v3 on v2

--- a/solution.py
+++ b/solution.py
@@ -34,9 +34,9 @@
 def kernel(
     left_ref, right_ref, lgrad_ref, rgrad_ref, loss_ref,
     lin, rin, lg, rg, lall, rall, er, ec, w, rm_s, rl_s, cm_s, cs_s, rp, ap,
-    row_stat, col_stat, bs, br, sib_s, sib_r, zs, zr, zm, part_a, part_b,
+    row_stat, col_stat, bs, br, ls, lr, sib_s, sib_r, zs, zr, zm, part_a, part_b,
     s_in, s_l, r_l, s_sib, r_sib, s_r, r_r, s_f, s_row, r_row, s_col, r_col,
-    s_gb, r_gb, s_gs, r_gs, s_gz, r_gz, r_gm, s_pa, r_pa, s_pb, r_pb,
+    s_gb, r_gb, s_gl, r_gl, s_gs, r_gs, s_gz, r_gz, r_gm, s_pa, r_pa, s_pb, r_pb,
 ):
     me = lax.axis_index("dp")
     core = me % 2
@@ -79,12 +79,9 @@
     c_left.start()
     c_right.start()
     barrier = pltpu.get_barrier_semaphore()
-    for i in range(G - 1):
-        da, db = PLANE_OFFS[i]
-        dev = plane_dev((a + da) % NA, (b + db) % NA)
-        pl.semaphore_signal(barrier, inc=1, device_id=dev, device_id_type=MESH)
-        dz, dc = LINE_OFFS[i]
-        dev = line_dev((z + dz) % NZ, (core + dc) % 2)
+    firsts = [plane_dev((a + d) % NA, b) for d in A_OFFS] + [plane_dev(a, (b + d) % NA) for d in A_OFFS]
+    firsts += [line_dev(zz(d), core) for d in (2, -2, 1, -1)] + [line_dev(z, other)]
+    for dev in firsts:
         pl.semaphore_signal(barrier, inc=1, device_id=dev, device_id_type=MESH)
     c_left.wait()
     c_right.wait()
@@ -93,7 +90,7 @@
     lg[q] = lbf
     rg[p] = rbf
     matched = jnp.sum(lbf.astype(jnp.float32) * rbf.astype(jnp.float32)) * scale
-    pl.semaphore_wait(barrier, 2 * (G - 1))
+    pl.semaphore_wait(barrier, len(firsts))
 
     def line_slot(k, c):
         return lg.at[k * 2 + c]
@@ -214,6 +211,9 @@
     col_loc = lax.broadcasted_iota(jnp.int32, (1, B), 1) - p * ROWS
     col_loc = jnp.where((col_loc >= 0) & (col_loc < ROWS), col_loc, -2)
 
+    for i, d in enumerate(A_OFFS):
+        go(part_b.at[p], part_b.at[p], s_pb.at[i], r_pb.at[p], plane_dev(a, (b + d) % NA))
+    go(part_a.at[q], part_a.at[q], s_pa.at[0], r_pa.at[q], line_dev(z, other))
     @pl.loop(0, CHUNKS)
     def _(t):
         at = pl.ds(pl.multiple_of(t * TM, TM), TM)
@@ -223,32 +223,20 @@
         ww = er[at, :] * rm_s[at, 0:1] + ec[at, :] * fc
         w[at, :] = jnp.where(row_loc == col_loc, ww - 2.0, ww).astype(jnp.bfloat16)
 
-    first = 0
-    for u in range(B // TN):
+    def right_step(u):
         rp[u * TN : (u + 1) * TN, :] = lax.dot_general(
             w[:, u * TN : (u + 1) * TN], lall[...], (((0,), (0,)), ((), ())), preferred_element_type=jnp.float32
         )
-        last = (u + 1) * TN // ROWS
-
-        @pl.loop(first, last)
-        def _(k):
-            piece = rp[pl.ds(pl.multiple_of(k * ROWS, ROWS), ROWS), :]
-            bs[k] = piece.astype(jnp.bfloat16)
-
-            @pl.when(k != p)
+        for k in range(u * TN // ROWS, (u + 1) * TN // ROWS):
+            ka, kb = k // NA, k % NA
+
+            @pl.when(ka != a)
             def _():
-                copy(bs.at[k], br.at[p], s_gb.at[k], r_gb.at[p], plane_dev(k // NA, k % NA)).start()
-
-            @pl.when(k == p)
-            def _():
-                rgrad_ref[...] = piece
-
-        first = last
-
-    @pl.loop(0, CHUNKS)
-    def _(o):
-        back = 3 - o
-        shift = (back % 2) * (1 - back // 2) * near - (back // 2) * (1 - back % 2) * near + (back // 2) * (back % 2) * 2
+                bs[k] = rp[k * ROWS : (k + 1) * ROWS, :].astype(jnp.bfloat16)
+                mine = a * NA + kb
+                copy(bs.at[k], br.at[mine], s_gb.at[k], r_gb.at[mine], plane_dev(ka, b)).start()
+
+    def left_step(shift):
         t = (zp + shift + CHUNKS) % CHUNKS
         at = pl.ds(pl.multiple_of(t * TM, TM), TM)
         part = jnp.dot(w[at, :], rall[...], preferred_element_type=jnp.float32)
@@ -256,10 +244,8 @@
             k = 2 * t + j
             lo = part[2 * j * ROWS : (2 * j + 1) * ROWS, :]
             hi = part[(2 * j + 1) * ROWS : (2 * j + 2) * ROWS, :]
-            mine = jnp.where(core == 0, lo, hi)
-            yours = jnp.where(core == 0, hi, lo)
-            ap[k] = mine
-            sib_s[k] = yours.astype(jnp.bfloat16)
+            ap[k] = jnp.where(core == 0, lo, hi)
+            sib_s[k] = jnp.where(core == 0, hi, lo).astype(jnp.bfloat16)
             copy(sib_s.at[k], sib_r.at[k], s_gs.at[k], r_gs.at[k], line_dev(z, other)).start()
 
     def chip_sum(k):
@@ -278,9 +264,28 @@
         zs[i] = value.astype(jnp.bfloat16)
         go(zs.at[i], zr.at[i - 3], s_gz.at[i], r_gz.at[i - 3], line_dev(zz(d), core))
 
+    right_step(0)
+    left_step(2)
+    right_step(1)
+    left_step(near)
+    for d in A_OFFS:
+        k = a * NA + (b + d) % NA
+        copy(part_b.at[p], part_b.at[k], s_pb.at[0], r_pb.at[k], plane_dev(0, 0)).wait_recv()
+    own = pl.ds(a * NA, NA)
+    for i, d in enumerate(A_OFFS):
+        dev = plane_dev((a + d) % NA, b)
+        go(part_b.at[own], part_b.at[own], s_pb.at[3 + i], r_pa.at[G + a], dev)
+    k = z * 2 + other
+    copy(part_a.at[q], part_a.at[k], s_pa.at[0], r_pa.at[k], line_dev(z, other)).wait_recv()
+    own = pl.ds(z * 2, 2)
+    for i, d in enumerate((4, 3, -3, 2, -2, 1, -1)):
+        go(part_a.at[own], part_a.at[own], s_pa.at[1 + i], r_pa.at[2 * G + z], line_dev(zz(d), core))
+    right_step(2)
     mid(0, 4, -2 * sg)
     mid(1, -3 * sg, -sg)
     mid(2, 3 * sg, sg)
+    left_step(-near)
+    left_step(0)
     end(3, 1, chip_sum(zz(1)))
     end(4, -1, chip_sum(zz(-1)))
     plus = chip_sum(zz(2 * sg))
@@ -288,32 +293,34 @@
     lgrad_ref[...] = chip_sum(z)
     end(5, 2 * sg, plus + mid_wait(2))
     end(6, -2 * sg, minus + mid_wait(0) + mid_wait(1))
-
-    for i in range(G - 1):
-        da, db = PLANE_OFFS[i]
-        dev = plane_dev((a + da) % NA, (b + db) % NA)
-        go(part_b.at[p], part_b.at[p], s_pb.at[i], r_pb.at[p], dev)
-        dz, dc = LINE_OFFS[i]
-        dev = line_dev((z + dz) % NZ, (core + dc) % 2)
-        go(part_a.at[q], part_a.at[q], s_pa.at[i], r_pa.at[q], dev)
-    for da, db in reversed(PLANE_OFFS):
-        ka, kb = (a + da) % NA, (b + db) % NA
-        k = ka * NA + kb
-        copy(bs.at[k], br.at[k], s_gb.at[k], r_gb.at[k], plane_dev(ka, kb)).wait()
-        rgrad_ref[...] += br[k].astype(jnp.float32)
-    for i in range(G - 1):
-        da, db = PLANE_OFFS[i]
-        ka, kb = (a + da) % NA, (b + db) % NA
-        k = ka * NA + kb
-        copy(part_b.at[p], part_b.at[k], s_pb.at[i], r_pb.at[k], plane_dev(ka, kb)).wait_recv()
-        dz, dc = LINE_OFFS[i]
-        kz, kc = (z + dz) % NZ, (core + dc) % 2
-        k = kz * 2 + kc
-        copy(part_a.at[q], part_a.at[k], s_pa.at[i], r_pa.at[k], line_dev(kz, kc)).wait_recv()
-    loss_ref[...] = (jnp.sum(part_a[...], axis=0) + jnp.sum(part_b[...], axis=0)) * (LN2 / (2.0 * NZ * 2 * B))
+    def right_sum(kb):
+        k = a * NA + kb
+        total = rp[pl.ds(pl.multiple_of(k * ROWS, ROWS), ROWS), :]
+        for d in A_OFFS:
+            k = (a + d) % NA * NA + kb
+            copy(bs.at[k], br.at[k], s_gb.at[k], r_gb.at[k], plane_dev(0, 0)).wait()
+            total += br[k].astype(jnp.float32)
+        return total
+
+    for i, d in enumerate(A_OFFS):
+        kb = (b + d) % NA
+        ls[i] = right_sum(kb).astype(jnp.bfloat16)
+        go(ls.at[i], lr.at[b], s_gl.at[i], r_gl.at[b], plane_dev(a, kb))
+    rgrad_ref[...] = right_sum(b)
+    for i, d in enumerate(A_OFFS):
+        copy(ls.at[i], lr.at[(b + d) % NA], s_gl.at[i], r_gl.at[(b + d) % NA], plane_dev(0, 0)).wait_recv()
+        rgrad_ref[...] += lr[(b + d) % NA].astype(jnp.float32)
     for i in range(4):
         copy(zs.at[3 + i], zr.at[i], s_gz.at[i], r_gz.at[i], line_dev(z, other)).wait_recv()
         lgrad_ref[...] += zr[i].astype(jnp.float32)
+    for d in A_OFFS:
+        k = (a + d) % NA
+        there = part_b.at[pl.ds(k * NA, NA)]
+        copy(there, there, s_pb.at[0], r_pa.at[G + k], plane_dev(0, 0)).wait_recv()
+    for d in (4, 3, -3, 2, -2, 1, -1):
+        there = part_a.at[pl.ds(zz(d) * 2, 2)]
+        copy(there, there, s_pa.at[0], r_pa.at[2 * G + zz(d)], line_dev(0, 0)).wait_recv()
+    loss_ref[...] = (jnp.sum(part_a[...], axis=0) + jnp.sum(part_b[...], axis=0)) * (LN2 / (2.0 * NZ * 2 * B))
     for k in range(NZ):
         copy(sib_s.at[k], sib_r.at[k], s_gs.at[k], r_gs.at[k], line_dev(z, other)).wait_send()
     for c in sends:
@@ -350,6 +357,8 @@
             pltpu.VMEM((G, 1, B + 128), f32),
             pltpu.VMEM((G, ROWS, D), bf16),
             pltpu.VMEM((G, ROWS, D), bf16),
+            pltpu.VMEM((3, ROWS, D), bf16),
+            pltpu.VMEM((NA, ROWS, D), bf16),
             pltpu.VMEM((NZ, ROWS, D), bf16),
             pltpu.VMEM((NZ, ROWS, D), bf16),
             pltpu.VMEM((7, ROWS, D), bf16),
@@ -365,9 +374,10 @@
             dma((G,)), dma((G,)),
             dma((G,)), dma((G,)),
             dma((G,)), dma((G,)),
+            dma((3,)), dma((NA,)),
             dma((NZ,)), dma((NZ,)),
             dma((7,)), dma((4,)), dma((3,)),
-            dma((G,)), dma((G,)),
+            dma((G,)), dma((3 * G,)),
             dma((G,)), dma((G,)),
         ],
         compiler_params=pltpu.CompilerParams(

time: 54.3 us -> 50.5 us (0.930)
  the two profiles are of different devices: /device:TPU:1 before, /device:TPU:30 now
where the time goes in v3:
time: 50.5 us; the launch traced here: 50.4 us
  Pallas kernels  47.3 us (94%)
  between operations  1.8 us (4%)
  local copies, waits for them, and re-layouts  1.29 us (3%)
    pallas_call x1, Pallas kernels, shards(): pl.pallas_call(kernel, out_shape=(pltpu.VMEM((ROWS, D), f32), pltpu.VMEM(...  47.3 us
    unnamed x2, local copies, waits for them, and re-layouts  1.29 us

profile of v3, /device:TPU:30, one launch (start us, length us, event | category | flops | bytes accessed | tf_op | source)
XLA Modules:
  0.0 50.4 jit_solution(15197961694367147984)
XLA Ops:
  0.6 47.3 %infonce.1 = (f32[72,384]{1,0:T(8,128)S(1)}, f32[72,384]{1,0:T(8,128)S(1)}, f32[1,128]{1,0:T(1,128)S(1)}) custom-call(f32[72,384]{1,0:T(8,128)} %left_ref.1, f32[72,384]{1,0:T(8,128)} %right_ref.1), custom_call_target="tpu_custom_call" | custom-call | flops 3057647616 | bytes 442368 | tf_op jit(solution)/shard_map/infonce/pallas_call | solution.py:335
  48.0 0.6 %copy.8 = f32[72,384]{1,0:T(8,128)} copy(f32[72,384]{1,0:T(8,128)S(1)} %get-tuple-element.9) | data formatting | bytes 221184
  48.6 0.6 %copy.9 = f32[72,384]{1,0:T(8,128)} copy(f32[72,384]{1,0:T(8,128)S(1)} %get-tuple-element.10) | data formatting | bytes 221184

commit v4 on v3

v4 whole, which is shorter than its diff:
```python
import math

import jax
import jax.numpy as jnp
from jax import lax
from jax.experimental import pallas as pl
from jax.experimental.pallas import tpu as pltpu
from jax.sharding import PartitionSpec as P

MESH = pl.DeviceIdType.MESH
NZ = 8
NA = 4
G = 16
ROWS = 72
D = 384
B = G * ROWS
TM = 4 * ROWS
CHUNKS = B // TM
TN = 384
LOG2E = math.log2(math.e)
LN2 = math.log(2.0)

A_OFFS = (2, 1, 3)
BUNDLES = (2, 1, 3, 0)
PLACE = (3, 1, 0, 2)
NEAR_FIRST = (1, 2, 0, 3)
PLANE_OFFS = sorted(
    [(i, j) for i in range(NA) for j in range(NA) if (i, j) != (0, 0)],
    key=lambda o: -(min(o[0], NA - o[0]) + min(o[1], NA - o[1])),
)
LINE_OFFS = sorted(
    [(i, j) for i in range(NZ) for j in range(2) if (i, j) != (0, 0)],
    key=lambda o: -min(o[0], NZ - o[0]),
)


def kernel(
    left_ref, right_ref, lgrad_ref, rgrad_ref, loss_ref,
    lin, rin, lg, rg, lall, rall, er, ec, w, rm_s, rl_s, cm_s, cs_s, rp, ap,
    row_stat, col_stat, bs, br, ls, lr, sib_s, sib_r, zs, zr, zm, part_a, part_b,
    s_in, s_l, r_l, r_sib, s_r, r_r, r_far, s_row, r_row, s_col, r_col,
    s_gb, r_gb, s_gl, r_gl, s_gs, r_gs, s_gz, r_gz, r_gm, s_pa, r_pa, s_pb, r_pb,
):
    me = lax.axis_index("dp")
    core = me % 2
    x = (me // 2) % NA
    y = (me // (2 * NA)) % NA
    z = me // (2 * G)
    a = y * (1 - core) + x * core
    b = x * (1 - core) + y * core
    step_a = 8 - 6 * core
    step_b = 2 + 6 * core
    p = a * NA + b
    mine = 3 * NA + b
    q = z * 2 + core
    here = 3 * 2 + core
    other = 1 - core
    sg = 1 - 2 * core
    scale = 2.0 / math.sqrt(D) * LOG2E

    def plane_dev(pa, pb):
        return (z * (2 * G) + pa * step_a + pb * step_b + core,)

    def line_dev(pz, pc):
        return (pz * (2 * G) + (y * NA + x) * 2 + pc,)

    def zz(d):
        return (z + d + NZ) % NZ

    def chip(d):
        return (d + 3 + NZ) % NZ


    def copy(src, dst, send, recv, dev):
        return pltpu.make_async_remote_copy(
            src_ref=src, dst_ref=dst, send_sem=send, recv_sem=recv, device_id=dev, device_id_type=MESH
        )

    def go(src, dst, send, recv, dev):
        copy(src, dst, send, recv, dev).start()

    def sent(like, send):
        copy(like, like, send, send, line_dev(z, other)).wait_send()

    def received(like, recv):
        copy(like, like, recv, recv, line_dev(z, other)).wait_recv()

    c_left = pltpu.make_async_copy(left_ref, lin, s_in.at[0])
    c_right = pltpu.make_async_copy(right_ref, rin, s_in.at[1])
    c_left.start()
    c_right.start()
    barrier = pltpu.get_barrier_semaphore()
    firsts = [plane_dev((a + d) % NA, b) for d in A_OFFS] + [plane_dev(a, (b + d) % NA) for d in A_OFFS]
    firsts += [line_dev(zz(d), core) for d in (2, -2, 1, -1)] + [line_dev(z, other)]
    for dev in firsts:
        pl.semaphore_signal(barrier, inc=1, device_id=dev, device_id_type=MESH)
    c_left.wait()
    c_right.wait()
    lbf = lin[...].astype(jnp.bfloat16)
    rbf = rin[...].astype(jnp.bfloat16)
    lg[here] = lbf
    rg[mine] = rbf
    matched = jnp.sum(lbf.astype(jnp.float32) * rbf.astype(jnp.float32)) * scale
    pl.semaphore_wait(barrier, len(firsts))

    def line_slot(d, c):
        return lg.at[chip(d) * 2 + c]

    def line_wait(d):
        received(lg.at[here], r_l.at[chip(d)])

    def line_send(of, d):
        go(line_slot(of, core), line_slot(of - d, core), s_l, r_l.at[chip(of - d)], line_dev(zz(d), core))

    def to_sibling(d):
        piece = line_slot(d, core)
        go(piece, piece, s_l, r_sib.at[chip(d)], line_dev(z, other))

    def plane_send(kb, d):
        src = rg.at[3 * NA + kb]
        there = PLACE[-d % NA] * NA + kb
        go(src, rg.at[there], s_r, r_far, plane_dev((a + d) % NA, b))

    for i, d in enumerate((2, -2, 1, -1)):
        line_send(0, d)
    for i, d in enumerate(A_OFFS):
        go(rg.at[mine], rg.at[mine], s_r, r_r.at[b], plane_dev(a, (b + d) % NA))
    for i, d in enumerate(A_OFFS):
        plane_send(b, d)
    to_sibling(0)
    for n, db in enumerate((1, 3, 2)):
        kb = (b + db) % NA
        received(rg.at[mine], r_r.at[kb])
        for i, d in enumerate(A_OFFS):
            plane_send(kb, d)
    line_wait(-2 * sg)
    line_send(-2 * sg, 2 * sg)
    line_send(-2 * sg, sg)
    line_wait(2 * sg)
    line_send(2 * sg, -sg)
    to_sibling(-2 * sg)
    to_sibling(2 * sg)
    for d in (1, -1, 3 * sg, -3 * sg, 4):
        line_wait(d)
        to_sibling(d)
    received(rg.at[pl.ds(0, 12)], r_far)

    def join(src, k, dst):
        two = [src[k].astype(jnp.float32), src[k + 1].astype(jnp.float32)]
        dst[k * ROWS : (k + 2) * ROWS, :] = jnp.concatenate(two, axis=0).astype(jnp.bfloat16)

    for k in range(0, G, 2):
        join(rg, k, rall)

    for t in NEAR_FIRST:
        for k in (2 * t, 2 * t + 1):
            received(lg.at[here], r_sib.at[k])
            join(lg, 2 * k, lall)
        at = slice(t * TM, (t + 1) * TM)
        s = lax.dot_general(
            lall[at, :], rall[...], (((1,), (1,)), ((), ())), preferred_element_type=jnp.float32
        ) * scale
        rm = jnp.max(s, axis=1, keepdims=True)
        e = jnp.exp2(s - rm)
        er[at, :] = e
        rm_s[at, :] = jnp.broadcast_to(rm, (TM, 128))
        rl_s[at, :] = jnp.broadcast_to(rm + jnp.log2(jnp.sum(e, axis=1, keepdims=True)), (TM, 128))
        cm = jnp.max(s, axis=0, keepdims=True)
        e = jnp.exp2(s - cm)
        ec[at, :] = e
        cm_s[t] = cm
        cs_s[t] = jnp.sum(e, axis=0, keepdims=True)

    cm = jnp.max(cm_s[...], axis=0)
    cs = jnp.sum(cs_s[...] * jnp.exp2(cm_s[...] - cm[None]), axis=0)
    col_stat[b, :, 0:B] = cm + jnp.log2(cs)
    col_stat[b, :, B : B + 128] = jnp.full((1, 128), matched, jnp.float32)
    rl = jnp.transpose(rl_s[...])[0:1, :]
    for k in range(NZ):
        row_stat[core, k : k + 1, :] = rl[:, k * 2 * ROWS : (k + 1) * 2 * ROWS]

    for i in range(G - 1):
        dz, dc = LINE_OFFS[i]
        dev = line_dev((z + dz) % NZ, (core + dc) % 2)
        there = (-dz % NZ) * 2 + core
        go(row_stat.at[core], row_stat.at[there], s_row, r_row, dev)
        da, db = PLANE_OFFS[i]
        dev = plane_dev((a + da) % NA, (b + db) % NA)
        there = (-da % NA) * NA + b
        go(col_stat.at[b], col_stat.at[there], s_col, r_col, dev)
    sent(rg.at[pl.ds(0, 15)], s_r)
    sent(lg.at[pl.ds(0, 15)], s_l)
    received(row_stat.at[pl.ds(0, 15)], r_row)
    received(col_stat.at[pl.ds(0, 15)], r_col)

    def combine(v):
        top = jnp.max(v, axis=0)
        return top + jnp.log2(jnp.sum(jnp.exp2(v - top[None]), axis=0))

    rows = [combine(row_stat[2 * d : 2 * d + 2]) for d in range(NZ)]
    rows = [v if d == 0 else jnp.concatenate([v[NZ - d :], v[: NZ - d]], axis=0) for d, v in enumerate(rows)]
    rows = combine(jnp.stack(rows))
    row_lse = jnp.concatenate([rows[k : k + 1, :] for k in range(NZ)], axis=1)

    def in_order(d):
        v = combine(col_stat[d * NA : (d + 1) * NA, :, 0:B])
        if d == 0:
            return v
        places = [PLACE[(off - d) % NA] * TM for off in BUNDLES]
        return jnp.concatenate([v[:, at : at + TM] for at in places], axis=1)

    col_lse = combine(jnp.stack([in_order(d) for d in range(NA)]))
    rm_s[...] = jnp.exp2(rm_s[...] - jnp.transpose(jnp.broadcast_to(row_lse, (128, B))))

    pairs = jnp.sum(col_stat[:, :, B : B + 128], axis=0)
    part_a[q] = jnp.sum(col_lse) - 2.0 * pairs
    part_b[p] = jnp.full((1, 128), jnp.sum(row_lse), jnp.float32)

    col_loc = lax.broadcasted_iota(jnp.int32, (1, B), 1) - mine * ROWS
    col_loc = jnp.where((col_loc >= 0) & (col_loc < ROWS), col_loc, -2)

    for i, d in enumerate(A_OFFS):
        go(part_b.at[p], part_b.at[p], s_pb, r_pb.at[0], plane_dev(a, (b + d) % NA))
    go(part_a.at[q], part_a.at[q], s_pa, r_pa.at[0], line_dev(z, other))
    for t in range(CHUNKS):
        at = slice(t * TM, (t + 1) * TM)
        fc = jnp.exp2(cm_s[t] - col_lse)
        row_loc = lax.broadcasted_iota(jnp.int32, (TM, 1), 0) + (t * TM - here * ROWS)
        row_loc = jnp.where((row_loc >= 0) & (row_loc < ROWS), row_loc, -1)
        ww = er[at, :] * rm_s[at, 0:1] + ec[at, :] * fc
        w[at, :] = jnp.where(row_loc == col_loc, ww - 2.0, ww).astype(jnp.bfloat16)

    def right_step(u):
        rp[u * TN : (u + 1) * TN, :] = lax.dot_general(
            w[:, u * TN : (u + 1) * TN], lall[...], (((0,), (0,)), ((), ())), preferred_element_type=jnp.float32
        )
        for k in range(u * TN // ROWS, (u + 1) * TN // ROWS):
            d = BUNDLES[k // NA]
            if d:
                bs[k] = rp[k * ROWS : (k + 1) * ROWS, :].astype(jnp.bfloat16)
                there = PLACE[-d % NA] * NA + k % NA
                go(bs.at[k], br.at[there], s_gb, r_gb.at[k % NA], plane_dev((a + d) % NA, b))

    def left_step(t):
        part = jnp.dot(w[t * TM : (t + 1) * TM, :], rall[...], preferred_element_type=jnp.float32)
        for j in range(2):
            k = 2 * t + j
            lo = part[2 * j * ROWS : (2 * j + 1) * ROWS, :]
            hi = part[(2 * j + 1) * ROWS : (2 * j + 2) * ROWS, :]
            ap[k] = jnp.where(core == 0, lo, hi)
            sib_s[k] = jnp.where(core == 0, hi, lo).astype(jnp.bfloat16)
            go(sib_s.at[k], sib_r.at[k], s_gs, r_gs.at[k], line_dev(z, other))

    def chip_sum(k):
        received(sib_r.at[0], r_gs.at[k])
        return ap[k] + sib_r[k].astype(jnp.float32)

    def mid(i, owner, d):
        zs[i] = chip_sum(chip(owner)).astype(jnp.bfloat16)
        go(zs.at[i], zm.at[i], s_gz, r_gm.at[i], line_dev(zz(d), core))

    def mid_wait(i):
        received(zm.at[i], r_gm.at[i])
        return zm[i].astype(jnp.float32)

    def end(i, d, value):
        zs[i] = value.astype(jnp.bfloat16)
        go(zs.at[i], zr.at[i - 3], s_gz, r_gz.at[i - 3], line_dev(zz(d), core))

    left_step(3)
    right_step(0)
    left_step(0)
    right_step(1)
    mid(0, 4, -2 * sg)
    mid(1, -3 * sg, -sg)
    mid(2, 3 * sg, sg)
    received(part_b.at[pl.ds(0, 3)], r_pb.at[0])
    own = pl.ds(a * NA, NA)
    for i, d in enumerate(A_OFFS):
        dev = plane_dev((a + d) % NA, b)
        go(part_b.at[own], part_b.at[own], s_pb, r_pb.at[1], dev)
    received(part_a.at[q], r_pa.at[0])
    own = pl.ds(z * 2, 2)
    for i, d in enumerate((4, 3, -3, 2, -2, 1, -1)):
        go(part_a.at[own], part_a.at[own], s_pa, r_pa.at[1], line_dev(zz(d), core))
    right_step(2)
    left_step(2)
    left_step(1)
    end(3, 1, chip_sum(chip(1)))
    end(4, -1, chip_sum(chip(-1)))
    plus = chip_sum(chip(2 * sg))
    minus = chip_sum(chip(-2 * sg))
    lgrad_ref[...] = chip_sum(chip(0))
    end(5, 2 * sg, plus + mid_wait(2))
    end(6, -2 * sg, minus + mid_wait(0) + mid_wait(1))
    def right_sum(kb):
        k = 3 * NA + kb
        total = rp[pl.ds(pl.multiple_of(k * ROWS, ROWS), ROWS), :]
        received(bs.at[pl.ds(0, 3)], r_gb.at[kb])
        for k in range(3):
            total += br[k * NA + kb].astype(jnp.float32)
        return total

    for i, d in enumerate(A_OFFS):
        kb = (b + d) % NA
        ls[i] = right_sum(kb).astype(jnp.bfloat16)
        go(ls.at[i], lr.at[b], s_gl, r_gl.at[b], plane_dev(a, kb))
    rgrad_ref[...] = right_sum(b)
    sent(row_stat.at[pl.ds(0, 15)], s_row)
    sent(col_stat.at[pl.ds(0, 15)], s_col)
    sent(sib_s, s_gs)
    sent(bs, s_gb)
    for i, d in enumerate(A_OFFS):
        received(ls.at[i], r_gl.at[(b + d) % NA])
        rgrad_ref[...] += lr[(b + d) % NA].astype(jnp.float32)
    for i in range(4):
        received(zr.at[i], r_gz.at[i])
        lgrad_ref[...] += zr[i].astype(jnp.float32)
    received(part_b.at[pl.ds(0, 12)], r_pb.at[1])
    received(part_a.at[pl.ds(0, 14)], r_pa.at[1])
    loss_ref[...] = (jnp.sum(part_a[...], axis=0) + jnp.sum(part_b[...], axis=0)) * (LN2 / (2.0 * NZ * 2 * B))
    sent(zs, s_gz)
    sent(ls, s_gl)
    sent(part_b.at[pl.ds(0, 15)], s_pb)
    sent(part_a.at[pl.ds(0, 15)], s_pa)


def shards(left, right):
    f32, bf16 = jnp.float32, jnp.bfloat16
    anywhere = pl.BlockSpec(memory_space=pl.ANY)
    vmem = pl.BlockSpec(memory_space=pltpu.VMEM)
    dma = pltpu.SemaphoreType.DMA
    left_grad, right_grad, loss = pl.pallas_call(
        kernel,
        out_shape=(pltpu.VMEM((ROWS, D), f32), pltpu.VMEM((ROWS, D), f32), pltpu.VMEM((1, 128), f32)),
        in_specs=[anywhere, anywhere],
        out_specs=(vmem, vmem, vmem),
        scratch_shapes=[
            pltpu.VMEM((ROWS, D), f32),
            pltpu.VMEM((ROWS, D), f32),
            pltpu.VMEM((G, ROWS, D), bf16),
            pltpu.VMEM((G, ROWS, D), bf16),
            pltpu.VMEM((B, D), bf16),
            pltpu.VMEM((B, D), bf16),
            pltpu.VMEM((B, B), f32),
            pltpu.VMEM((B, B), f32),
            pltpu.VMEM((B, B), bf16),
            pltpu.VMEM((B, 128), f32),
            pltpu.VMEM((B, 128), f32),
            pltpu.VMEM((CHUNKS, 1, B), f32),
            pltpu.VMEM((CHUNKS, 1, B), f32),
            pltpu.VMEM((B, D), f32),
            pltpu.VMEM((NZ, ROWS, D), f32),
            pltpu.VMEM((G, NZ, 2 * ROWS), f32),
            pltpu.VMEM((G, 1, B + 128), f32),
            pltpu.VMEM((12, ROWS, D), bf16),
            pltpu.VMEM((12, ROWS, D), bf16),
            pltpu.VMEM((3, ROWS, D), bf16),
            pltpu.VMEM((NA, ROWS, D), bf16),
            pltpu.VMEM((NZ, ROWS, D), bf16),
            pltpu.VMEM((NZ, ROWS, D), bf16),
            pltpu.VMEM((7, ROWS, D), bf16),
            pltpu.VMEM((4, ROWS, D), bf16),
            pltpu.VMEM((3, ROWS, D), bf16),
            pltpu.VMEM((G, 1, 128), f32),
            pltpu.VMEM((G, 1, 128), f32),
            dma((2,)),
            dma, dma((NZ,)), dma((NZ,)),
            dma, dma((NA,)), dma,
            dma, dma,
            dma, dma,
            dma, dma((NA,)),
            dma, dma((NA,)),
            dma, dma((NZ,)),
            dma, dma((4,)), dma((3,)),
            dma, dma((2,)),
            dma, dma((2,)),
        ],
        compiler_params=pltpu.CompilerParams(
            collective_id=0, has_side_effects=True, vmem_limit_bytes=56 * 2**20
        ),
        cost_estimate=pl.CostEstimate(flops=6 * B * B * D, bytes_accessed=16 * ROWS * D, transcendentals=2 * B * B),
        name="infonce",
    )(left, right)
    return left_grad, right_grad, loss[0, 0]


def solution(mesh):
    return jax.shard_map(
        shards,
        mesh=mesh,
        in_specs=(P("dp", None), P("dp", None)),
        out_specs=(P("dp", None), P("dp", None), P()),
        check_vma=False,
    )
```

time: 50.5 us -> 46.7 us (0.925)
  the two profiles are of different devices: /device:TPU:30 before, /device:TPU:1 now
where the time goes in v4:
time: 46.7 us; the launch traced here: 46.5 us
  Pallas kernels  43.4 us (93%)
  between operations  1.8 us (4%)
  local copies, waits for them, and re-layouts  1.29 us (3%)
    pallas_call x1, Pallas kernels, shards(): pl.pallas_call(kernel, out_shape=(pltpu.VMEM((ROWS, D), f32), pltpu.VMEM(...  43.4 us
    unnamed x2, local copies, waits for them, and re-layouts  1.29 us

profile of v4, /device:TPU:1, one launch (start us, length us, event | category | flops | bytes accessed | tf_op | source)
XLA Modules:
  0.0 46.5 jit_solution(5024316979184662321)
XLA Ops:
  0.6 43.4 %infonce.1 = (f32[72,384]{1,0:T(8,128)S(1)}, f32[72,384]{1,0:T(8,128)S(1)}, f32[1,128]{1,0:T(1,128)S(1)}) custom-call(f32[72,384]{1,0:T(8,128)} %left_ref.1, f32[72,384]{1,0:T(8,128)} %right_ref.1), custom_call_target="tpu_custom_call" | custom-call | flops 3057647616 | bytes 442368 | tf_op jit(solution)/shard_map/infonce/pallas_call | solution.py:333
  44.1 0.6 %copy.8 = f32[72,384]{1,0:T(8,128)} copy(f32[72,384]{1,0:T(8,128)S(1)} %get-tuple-element.9) | data formatting | bytes 221184
  44.7 0.6 %copy.9 = f32[72,384]{1,0:T(8,128)} copy(f32[72,384]{1,0:T(8,128)S(1)} %get-tuple-element.10) | data formatting | bytes 221184

commit v5 on v4

--- a/solution.py
+++ b/solution.py
@@ -35,12 +35,14 @@
 
 
 def kernel(
-    left_ref, right_ref, lgrad_ref, rgrad_ref, loss_ref,
+    left_ref, right_ref, out_ref,
     lin, rin, lg, rg, lall, rall, er, ec, w, rm_s, rl_s, cm_s, cs_s, rp, ap,
     row_stat, col_stat, bs, br, ls, lr, sib_s, sib_r, zs, zr, zm, part_a, part_b,
     s_in, s_l, r_l, r_sib, s_r, r_r, r_far, s_row, r_row, s_col, r_col,
     s_gb, r_gb, s_gl, r_gl, s_gs, r_gs, s_gz, r_gz, r_gm, s_pa, r_pa, s_pb, r_pb,
 ):
+    lgrad_ref, rgrad_ref = out_ref.at[pl.ds(0, ROWS)], out_ref.at[pl.ds(ROWS, ROWS)]
+    loss_ref = out_ref.at[pl.ds(2 * ROWS, 1), pl.ds(0, 128)]
     me = lax.axis_index("dp")
     core = me % 2
     x = (me // 2) % NA
@@ -330,11 +332,11 @@
     anywhere = pl.BlockSpec(memory_space=pl.ANY)
     vmem = pl.BlockSpec(memory_space=pltpu.VMEM)
     dma = pltpu.SemaphoreType.DMA
-    left_grad, right_grad, loss = pl.pallas_call(
+    out = pl.pallas_call(
         kernel,
-        out_shape=(pltpu.VMEM((ROWS, D), f32), pltpu.VMEM((ROWS, D), f32), pltpu.VMEM((1, 128), f32)),
+        out_shape=pltpu.VMEM((2 * ROWS + 8, D), f32),
         in_specs=[anywhere, anywhere],
-        out_specs=(vmem, vmem, vmem),
+        out_specs=vmem,
         scratch_shapes=[
             pltpu.VMEM((ROWS, D), f32),
             pltpu.VMEM((ROWS, D), f32),
@@ -382,7 +384,7 @@
         cost_estimate=pl.CostEstimate(flops=6 * B * B * D, bytes_accessed=16 * ROWS * D, transcendentals=2 * B * B),
         name="infonce",
     )(left, right)
-    return left_grad, right_grad, loss[0, 0]
+    return out[:ROWS], out[ROWS : 2 * ROWS], out[2 * ROWS, 0]
 
 
 def solution(mesh):

time: 46.7 us -> 45.4 us (0.972)
  between operations: 1.8 us -> 0.64 us
    unnamed x2 -> x0, local copies, waits for them, and re-layouts: 1.29 us -> none
    slice x0 -> x2, local copies, waits for them, and re-layouts: none -> 1.21 us  [shards(): return (out[:ROWS], out[ROWS:2 * ROWS], out[2 * ROWS, 0])]
where the time goes in v5:
time: 45.4 us; the launch traced here: 45.3 us
  Pallas kernels  43.4 us (96%)
  local copies, waits for them, and re-layouts  1.21 us (3%)
  between operations  0.64 us (1%)
    pallas_call x1, Pallas kernels, shards(): pl.pallas_call(kernel, out_shape=pltpu.VMEM((2 * ROWS + 8, D), f32), in_s...  43.4 us
    slice x2, local copies, waits for them, and re-layouts, shards(): return (out[:ROWS], out[ROWS:2 * ROWS], out[2 * ROWS, 0])  1.21 us

profile of v5, /device:TPU:1, one launch (start us, length us, event | category | flops | bytes accessed | tf_op | source)
XLA Modules:
  0.0 45.3 jit_solution(6113730048874989037)
XLA Ops:
  0.6 43.4 %infonce.1 = f32[152,384]{1,0:T(8,128)S(1)} custom-call(f32[72,384]{1,0:T(8,128)} %left_ref.1, f32[72,384]{1,0:T(8,128)} %right_ref.1), custom_call_target="tpu_custom_call" | custom-call | flops 3057647616 | bytes 442368 | tf_op jit(solution)/shard_map/infonce/pallas_call | solution.py:335
  44.1 0.7 %fusion = (f32[72,384]{1,0:T(8,128)}, f32[72,384]{1,0:T(8,128)}) fusion(f32[152,384]{1,0:T(8,128)S(1)} %infonce.1), kind=kLoop, calls=%fused_computation | loop fusion | bytes 442368 | tf_op jit(solution)/shard_map/slice | solution.py:387
  44.8 0.5 %slice.11 = f32[1,1]{1,0:T(1,128)} slice(f32[152,384]{1,0:T(8,128)S(1)} %infonce.1), slice={[144:145], [0:1]} | slice | bytes 8 | tf_op jit(solution)/shard_map/slice | solution.py:387

commit v6 on v5

--- a/solution.py
+++ b/solution.py
@@ -89,20 +89,19 @@
 
     c_left = pltpu.make_async_copy(left_ref, lin, s_in.at[0])
     c_right = pltpu.make_async_copy(right_ref, rin, s_in.at[1])
-    c_left.start()
-    c_right.start()
     barrier = pltpu.get_barrier_semaphore()
     firsts = [plane_dev((a + d) % NA, b) for d in A_OFFS] + [plane_dev(a, (b + d) % NA) for d in A_OFFS]
     firsts += [line_dev(zz(d), core) for d in (2, -2, 1, -1)] + [line_dev(z, other)]
     for dev in firsts:
         pl.semaphore_signal(barrier, inc=1, device_id=dev, device_id_type=MESH)
+    c_left.start()
+    c_right.start()
     c_left.wait()
     c_right.wait()
     lbf = lin[...].astype(jnp.bfloat16)
     rbf = rin[...].astype(jnp.bfloat16)
     lg[here] = lbf
     rg[mine] = rbf
-    matched = jnp.sum(lbf.astype(jnp.float32) * rbf.astype(jnp.float32)) * scale
     pl.semaphore_wait(barrier, len(firsts))
 
     def line_slot(d, c):
@@ -130,6 +129,7 @@
     for i, d in enumerate(A_OFFS):
         plane_send(b, d)
     to_sibling(0)
+    matched = jnp.sum(lbf.astype(jnp.float32) * rbf.astype(jnp.float32)) * scale
     for n, db in enumerate((1, 3, 2)):
         kb = (b + db) % NA
         received(rg.at[mine], r_r.at[kb])

time: 45.4 us -> 45.4 us (level)
  no operation moved by 1% of the time
where the time goes in v6:
time: 45.4 us; the launch traced here: 45.3 us
  Pallas kernels  43.5 us (96%)
  local copies, waits for them, and re-layouts  1.21 us (3%)
  between operations  0.64 us (1%)
    pallas_call x1, Pallas kernels, shards(): pl.pallas_call(kernel, out_shape=pltpu.VMEM((2 * ROWS + 8, D), f32), in_s...  43.5 us
    slice x2, local copies, waits for them, and re-layouts, shards(): return (out[:ROWS], out[ROWS:2 * ROWS], out[2 * ROWS, 0])  1.21 us

profile of v6, /device:TPU:1, one launch (start us, length us, event | category | flops | bytes accessed | tf_op | source)
XLA Modules:
  0.0 45.3 jit_solution(14919801503596147132)
XLA Ops:
  0.6 43.5 %infonce.1 = f32[152,384]{1,0:T(8,128)S(1)} custom-call(f32[72,384]{1,0:T(8,128)} %left_ref.1, f32[72,384]{1,0:T(8,128)} %right_ref.1), custom_call_target="tpu_custom_call" | custom-call | flops 3057647616 | bytes 442368 | tf_op jit(solution)/shard_map/infonce/pallas_call | solution.py:335
  44.1 0.7 %fusion = (f32[72,384]{1,0:T(8,128)}, f32[72,384]{1,0:T(8,128)}) fusion(f32[152,384]{1,0:T(8,128)S(1)} %infonce.1), kind=kLoop, calls=%fused_computation | loop fusion | bytes 442368 | tf_op jit(solution)/shard_map/slice | solution.py:387
  44.8 0.5 %slice.11 = f32[1,1]{1,0:T(1,128)} slice(f32[152,384]{1,0:T(8,128)S(1)} %infonce.1), slice={[144:145], [0:1]} | slice | bytes 8 | tf_op jit(solution)/shard_map/slice | solution.py:387
